TPU v7x, 256 devices: a whole 4x4x8 slice. The times are simulated.
256 devices in a mesh: row: 8 (over x, y_hi), col: 32 (over z, y_lo, core).
Axes of the slice: x: 4, y: 4 (y_hi: 2, y_lo: 2; y = y_hi * 2 + y_lo), z: 8, core: 2. Of those that a mesh axis runs over, the one named last changes fastest.
Arguments:
- matrix: float32 [3, 8, 128, 32, 32, 128], P(None, 'row', None, None, 'col'), may hold values from -6 to 6
- factors: float32 [10, 512, 512], P(None, None, 'col'), as said below
- starts: int32 [10], replicated, may hold values from 0 to 2560, as said below
Outputs:
- updated: float32 [3, 8, 128, 32, 32, 128], P(None, 'row', None, None, 'col')
Inputs may be any that keep to these rules, and one draw needn't show every extreme that they name: starts[w] = starts[0] + 256 * w, and starts[0] is a multiple of 128. Each factors[w] is orthogonal.
All inputs are finite; a program needn't handle non-finite values.
Results may differ from a plain program's by a relative error of at most 0.0001.
Values sent between devices are 32-bit elements; how exact they have to be, the bound alone decides.
A program may use at most 128 MiB of HBM per device.

v0:
```python
import jax
import jax.numpy as jnp
from jax import lax
from jax.sharding import PartitionSpec as P

WIN = 512
SHIFT = 256
WINS = 10


def pick_tiles(first_tile, per_device, axis_count, position, span_tiles):
    global_tiles = (
        first_tile
        + jnp.remainder(position - first_tile, axis_count)
        + jnp.arange(per_device, dtype=jnp.int32) * axis_count
    )
    tile_valid = global_tiles < first_tile + span_tiles
    return (tile_valid, jnp.where(tile_valid, global_tiles // axis_count, 0))


def band_order(first_tile, axis_count, per_device, span_tiles):
    places = jnp.arange(span_tiles, dtype=jnp.int32)
    return jnp.remainder(first_tile + places, axis_count) * per_device + places // axis_count


def slot_order(first_tile, axis_count, per_device, span_tiles):
    slot_ids = jnp.arange(axis_count * per_device, dtype=jnp.int32)
    places = (
        jnp.remainder(slot_ids // per_device - first_tile, axis_count)
        + slot_ids % per_device * axis_count
    )
    slot_valid = places < span_tiles
    return (slot_valid, jnp.where(slot_valid, places, 0))


def body(matrix, factors, starts):
    row_count = lax.axis_size("row")
    col_count = lax.axis_size("col")
    row_place = lax.axis_index("row")
    col_place = lax.axis_index("col")
    row_cycles = matrix.shape[0]
    tile_size = matrix.shape[2]
    col_cycles = matrix.shape[3]
    span_tiles = (WIN + SHIFT * (WINS - 1)) // tile_size
    first_tile = starts[0] // tile_size
    all_factors = lax.all_gather(factors, "col", axis=2, tiled=True)

    def left_step(window, band_rows):
        offset_row = starts[window] - starts[0]
        factor_now = lax.dynamic_index_in_dim(all_factors, window, 0, keepdims=False)
        window_rows = lax.dynamic_slice_in_dim(band_rows, offset_row, WIN, 0)
        result_rows = jnp.dot(
            factor_now.T,
            window_rows,
            precision=lax.Precision.HIGHEST,
            preferred_element_type=jnp.float32,
        )
        return lax.dynamic_update_slice_in_dim(band_rows, result_rows, offset_row, 0)

    def right_step(window, band_cols):
        offset_col = starts[window] - starts[0]
        factor_now = lax.dynamic_index_in_dim(all_factors, window, 0, keepdims=False)
        window_cols = lax.dynamic_slice_in_dim(band_cols, offset_col, WIN, 1)
        result_cols = jnp.dot(
            window_cols,
            factor_now,
            precision=lax.Precision.HIGHEST,
            preferred_element_type=jnp.float32,
        )
        return lax.dynamic_update_slice_in_dim(band_cols, result_cols, offset_col, 1)

    local_tiles = matrix.reshape(row_cycles, tile_size, col_cycles * tile_size)
    rows_each = -(-span_tiles // row_count)
    row_valid, row_index = pick_tiles(first_tile, rows_each, row_count, row_place, span_tiles)
    picked = jnp.where(row_valid[:, None, None], jnp.take(local_tiles, row_index, axis=0), 0.0)
    received = lax.all_to_all(picked, "row", split_axis=2, concat_axis=0, tiled=True)
    band_rows = jnp.take(received, band_order(first_tile, row_count, rows_each, span_tiles), axis=0)
    band_rows = band_rows.reshape(span_tiles * tile_size, received.shape[2])
    band_rows = lax.fori_loop(0, WINS, left_step, band_rows)
    row_tiles = band_rows.reshape(span_tiles, tile_size, received.shape[2])
    send_valid, send_place = slot_order(first_tile, row_count, rows_each, span_tiles)
    backsend = jnp.where(send_valid[:, None, None], jnp.take(row_tiles, send_place, axis=0), 0.0)
    returned = lax.all_to_all(backsend, "row", split_axis=0, concat_axis=2, tiled=True)
    for member in range(rows_each):
        local_tiles = jnp.where(
            row_valid[member],
            lax.dynamic_update_index_in_dim(local_tiles, returned[member], row_index[member], 0),
            local_tiles,
        )
    local_rows = row_cycles * tile_size
    column_view = local_tiles.reshape(local_rows, col_cycles, tile_size)
    cols_each = -(-span_tiles // col_count)
    col_valid, col_index = pick_tiles(first_tile, cols_each, col_count, col_place, span_tiles)
    picked_cols = jnp.where(col_valid[None, :, None], jnp.take(column_view, col_index, axis=1), 0.0)
    col_order = band_order(first_tile, col_count, cols_each, span_tiles)
    gathered = lax.all_gather(picked_cols, "col", axis=1, tiled=True)
    band_cols = jnp.take(gathered, col_order, axis=1).reshape(local_rows, span_tiles * tile_size)
    band_cols = lax.fori_loop(0, WINS, right_step, band_cols)
    own_places = (
        jnp.remainder(col_place - first_tile, col_count)
        + jnp.arange(cols_each, dtype=jnp.int32) * col_count
    )
    own_places = jnp.where(col_valid, own_places, 0)
    returned_cols = jnp.take(
        band_cols.reshape(local_rows, span_tiles, tile_size), own_places, axis=1
    )
    member = 0
    column_view = jnp.where(
        col_valid[member],
        lax.dynamic_update_index_in_dim(
            column_view, returned_cols[:, member], col_index[member], 1
        ),
        column_view,
    )
    return column_view.reshape(matrix.shape)


def solution(mesh):
    placed = (P(None, "row", None, None, "col", None), P(None, None, "col"), P())
    return jax.shard_map(
        body,
        mesh=mesh,
        in_specs=placed,
        out_specs=P(None, "row", None, None, "col", None),
        check_vma=False,
    )
```

profile of v0, /device:TPU:1, one launch (start us, length us, event | category | flops | bytes accessed | tf_op | source)
XLA Modules:
  0.0 615.0 jit_solution(2616811414107815150)
XLA Ops:
  10.4 19.2 %reduce.3 = f32[3,128,32,128]{3,2,1,0:T(8,128)} reduce(f32[3,1,128,32,1,128]{5,4,3,2,1,0:T(1,128)} %param.7, f32[]{:T(128)} %broadcast.920), dimensions={1,4}, to_apply=%param.7.reduce_sub_computation.3 | reduce | bytes 12582916 | tf_op args[0]
  29.6 7.2 %reshape.444 = f32[3,128,4096]{2,1,0:T(8,128)} reshape(f32[3,128,32,128]{3,2,1,0:T(8,128)} %reduce.3) | data formatting | bytes 12582912 | tf_op jit(solution)/shard_map/reshape | solution.py:72
  36.9 6.5 %gather_fusion = f32[3,128,4096]{2,1,0:T(8,128)} fusion(f32[3,128,4096]{2,1,0:T(8,128)} %reshape.444, s32[1024]{0:T(1024)S(1)} %pad_clamp_fusion.3), kind=kCustom, calls=%fused_computation | custom fusion | bytes 12582924 | tf_op jit(solution)/shard_map/jit(_take)/gather | solution.py:75
  43.5 6.8 %select_select_fusion.1 = f32[3,128,4096]{2,1,0:T(8,128)} fusion(f32[3,128,4096]{2,1,0:T(8,128)} %gather_fusion, pred[3]{0:T(512)(128)(4,1)S(1)} %get-tuple-element.227, pred[3]{0:T(512)(128)(4,1)S(1)} %get-tuple-element.244), kind=kLoop, calls=%fused_computation.15 | loop fusion | flops 3145728 | bytes 12582918 | tf_op jit(solution)/shard_map/jit(_where)/select_n | solution.py:75
  50.2 9.2 %copy.53 = f32[3,128,4096]{1,0,2:T(4,128)} copy(f32[3,128,4096]{2,1,0:T(8,128)} %select_select_fusion.1) | data formatting | bytes 12582912 | tf_op jit(solution)/shard_map/jit(_where)/select_n | solution.py:75
  59.5 7.5 %all-to-all-start = ((f32[3,128,4096]{1,0,2:T(4,128)}), f32[3,128,4096]{1,0,2:T(4,128)}, u32[]{:S(2)}, u32[]{:S(2)}) async-start(f32[3,128,4096]{1,0,2:T(4,128)} %copy.53), calls=%async_computation | async-start | bytes 16777216 | tf_op jit(solution)/shard_map/all_to_all | solution.py:76
  67.2 115.0 %all-to-all-done = f32[3,128,4096]{1,0,2:T(4,128)} async-done(((f32[3,128,4096]{1,0,2:T(4,128)}), f32[3,128,4096]{1,0,2:T(4,128)}, u32[]{:S(2)}, u32[]{:S(2)}) %all-to-all-start) | async-done | bytes 6291488 | tf_op jit(solution)/shard_map/all_to_all | solution.py:76
  182.2 6.5 %copy.54 = f32[3,128,4096]{1,2,0:T(8,128)} copy(f32[3,128,4096]{1,0,2:T(4,128)} %all-to-all-done) | data formatting | bytes 12582912 | tf_op jit(solution)/shard_map/all_to_all | solution.py:76
  188.7 6.6 %copy.55 = f32[8,3,128,512]{3,2,1,0:T(8,128)} copy(f32[8,3,128,512]{2,3,0,1:T(8,128)} %bitcast.80) | data formatting | bytes 12582912 | tf_op jit(solution)/shard_map/all_to_all | solution.py:76
  195.3 6.2 %gather_fusion.1 = f32[22,128,512]{2,1,0:T(8,128)} fusion(f32[24,128,512]{2,1,0:T(8,128)} %bitcast.81, s32[1024]{0:T(1024)S(1)} %pad_clamp_fusion.2), kind=kCustom, calls=%fused_computation.1 | custom fusion | bytes 11534424 | tf_op jit(solution)/shard_map/jit(_take)/gather | solution.py:77
  201.5 5.0 bitcast_select_fusion
  206.6 11.3 %copy.56 = f32[10,512,512]{2,1,0:T(8,128)} copy(f32[10,512,512]{1,2,0:T(8,128)} %all-gather.3.cloned.1.call-done) | data formatting | bytes 20971520 | tf_op jit(solution)/shard_map/while | solution.py:79
  217.9 92.9 %while.28 = (s32[]{:T(128)}, f32[2816,512]{1,0:T(8,128)}, f32[10,512,512]{2,1,0:T(8,128)}, s32[10]{0:T(128)S(1)}, s32[]{:T(128)}, /*index=5*/s32[]{:T(128)}, s32[]{:T(128)}) while((s32[]{:T(128)}, f32[2816,512]{1,0:T(8,128)}, f32[10,512,512]{2,1,0:T(8,128)}, s32[10]{0:T(128)S(1)}, s32[]{:T(128)}, /*index=5*/s32[]{:T(128)}, s32[]{:T(128)}) %tuple.93), condition=%wide.region_1.2_spmd, body=%wide.region_0.1_spmd.sunk | while | flops 1610612736 | bytes 5243543 | solution.py:79
  219.7 3.4 fusion.46
  223.1 4.1 dynamic_update_slice.22
  229.0 3.4 fusion.46
  232.4 4.1 dynamic_update_slice.22
  238.3 3.4 fusion.46
  241.8 4.2 dynamic_update_slice.22
  247.7 3.4 fusion.46
  251.1 4.2 dynamic_update_slice.22
  257.0 3.4 fusion.46
  260.5 4.1 dynamic_update_slice.22
  266.3 3.4 fusion.46
  269.8 4.2 dynamic_update_slice.22
  275.7 3.4 fusion.46
  279.1 4.1 dynamic_update_slice.22
  285.0 3.5 fusion.46
  288.5 4.2 dynamic_update_slice.22
  294.4 3.5 fusion.46
  297.9 4.1 dynamic_update_slice.22
  303.8 3.4 fusion.46
  307.2 3.5 dynamic_update_slice.22
  310.8 6.3 %gather_fusion.2 = f32[24,128,512]{2,1,0:T(8,128)} fusion(f32[22,128,512]{2,1,0:T(8,128)} %bitcast.79, s32[1024]{0:T(1024)S(1)} %pad_clamp_fusion.1), kind=kCustom, calls=%fused_computation.2 | custom fusion | bytes 12583008 | tf_op jit(solution)/shard_map/jit(_take)/gather | solution.py:82
  317.0 6.8 %select_select_fusion = f32[24,128,512]{2,1,0:T(8,128)} fusion(f32[24,128,512]{2,1,0:T(8,128)} %gather_fusion.2, pred[24]{0:T(512)(128)(4,1)S(1)} %get-tuple-element.242, pred[24]{0:T(512)(128)(4,1)S(1)} %get-tuple-element.243), kind=kLoop, calls=%fused_computation.14 | loop fusion | flops 3145728 | bytes 12582960 | tf_op jit(solution)/shard_map/jit(_where)/select_n | solution.py:82
  323.9 4.8 all-to-all-start.1
  336.2 78.9 %all-to-all-done.1 = f32[24,128,512]{2,1,0:T(8,128)} async-done(((f32[24,128,512]{2,1,0:T(8,128)}), f32[24,128,512]{2,1,0:T(8,128)}, u32[]{:S(2)}, u32[]{:S(2)}) %all-to-all-start.1) | async-done | bytes 6291488 | tf_op jit(solution)/shard_map/all_to_all | solution.py:83
  415.1 3.6 slice_bitcast_fusion
  429.6 72.6 %all-gather.5.cloned.1.call-done = f32[384,32,128]{2,0,1:T(8,128)} async-done(((f32[384,1,128]{2,0,1:T(8,128)}), f32[384,32,128]{2,0,1:T(8,128)}) %all-gather.5.cloned.1.call-update) | async-done | bytes 6291472 | tf_op jit(solution)/shard_map/all_gather | solution.py:96
  502.2 5.6 gather_fusion.3
  507.8 5.9 copy.61
  513.7 4.4 bitcast_select_fusion.1
  518.1 81.0 %while.29 = (s32[]{:T(128)}, f32[384,2816]{0,1:T(8,128)}, s32[10]{0:T(128)S(1)}, f32[10,512,512]{2,1,0:T(8,128)}, s32[]{:T(128)}, /*index=5*/s32[]{:T(128)}, s32[]{:T(128)}) while((s32[]{:T(128)}, f32[384,2816]{0,1:T(8,128)}, s32[10]{0:T(128)S(1)}, f32[10,512,512]{2,1,0:T(8,128)}, s32[]{:T(128)}, /*index=5*/s32[]{:T(128)}, s32[]{:T(128)}) %tuple.94), condition=%wide.region_3.4_spmd, body=%wide.region_2.3_spmd.sunk | while | flops 1207959552 | bytes 4194967 | solution.py:98
  520.0 3.3 fusion.50
  523.3 2.9 dynamic_update_slice.23
  528.1 3.3 fusion.50
  531.4 2.9 dynamic_update_slice.23
  536.1 3.3 fusion.50
  539.5 2.9 dynamic_update_slice.23
  544.2 3.3 fusion.50
  547.6 2.9 dynamic_update_slice.23
  552.3 3.3 fusion.50
  555.7 2.9 dynamic_update_slice.23
  560.5 3.3 fusion.50
  563.8 2.9 dynamic_update_slice.23
  568.6 3.3 fusion.50
  571.9 2.9 dynamic_update_slice.23
  576.7 3.3 fusion.50
  580.0 2.9 dynamic_update_slice.23
  584.8 3.3 fusion.50
  588.1 2.9 dynamic_update_slice.23
  592.9 3.3 fusion.50
  596.2 2.9 dynamic_update_slice.23
  601.8 6.4 %select_n.478 = f32[384,32,128]{2,1,0:T(8,128)} dynamic-update-slice(f32[384,32,128]{2,1,0:T(8,128)} %bitcast.89, f32[384,1,128]{2,1,0:T(1,128)S(1)} %broadcast_select_fusion.3, s32[]{:T(128)} %constant.284.clone.1, s32[]{:T(128)S(6)} %select_n.475, s32[]{:T(128)} %constant.284.clone.1) | dynamic-update-slice | bytes 393220 | tf_op jit(solution)/shard_map/jit(_where)/select_n | solution.py:108
  (62 shorter events, 28.2 us)
Async XLA Ops:
  6.5 200.0 %all-gather.3.cloned.1.call-start = ((), (), s32[]{:S(2)}) async-start(), calls=%async_computation.2 | async-start | bytes 10813440 | tf_op jit(solution)/shard_map/all_gather | solution.py:46
  59.5 122.7 %all-to-all-start = ((f32[3,128,4096]{1,0,2:T(4,128)}), f32[3,128,4096]{1,0,2:T(4,128)}, u32[]{:S(2)}, u32[]{:S(2)}) async-start(f32[3,128,4096]{1,0,2:T(4,128)} %copy.53), calls=%async_computation | async-start | bytes 16777216 | tf_op jit(solution)/shard_map/all_to_all | solution.py:76
  206.6 11.3 %copy-start.1 = (s32[10]{0:T(128)S(1)}, s32[10]{0:T(128)}, u32[]{:S(2)}) copy-start(s32[10]{0:T(128)} %param.9) | copy-start | bytes 124
  323.9 91.2 %all-to-all-start.1 = ((f32[24,128,512]{2,1,0:T(8,128)}), f32[24,128,512]{2,1,0:T(8,128)}, u32[]{:S(2)}, u32[]{:S(2)}) async-start(f32[24,128,512]{2,1,0:T(8,128)} %select_select_fusion), calls=%async_computation.1 | async-start | bytes 12582912 | tf_op jit(solution)/shard_map/all_to_all | solution.py:83
  328.6 173.6 %all-gather.5.cloned.1.call-start = ((), (), s32[]{:S(2)}) async-start(), calls=%async_computation.3 | async-start | bytes 6488064 | tf_op jit(solution)/shard_map/all_gather | solution.py:96
  418.7 2.2 slice-start
  418.9 2.7 slice-start.1
  425.9 2.7 copy-start
Sparse Core Ops, SparseCore 0:
  9.2 159.0 all-gather.2
  429.6 72.5 all-gather.4
where the time goes:
time: 619 us; the launch traced here: 615 us
  waiting for transfers between devices  267 us (43%)
  local copies, waits for them, and re-layouts  173 us (28%)
  matrix products  67.9 us (11%)
  other arithmetic  47.9 us (8%)
  loops' own time  24.7 us (4%)
  between operations  22.2 us (4%)
  starting transfers between devices  12.5 us (2%)
    all_to_all x1, waiting for transfers between devices, body(): lax.all_to_all(picked, 'row', split_axis=2, concat_axis=0, tiled=True)  115 us
    all_to_all x1, waiting for transfers between devices, body(): lax.all_to_all(backsend, 'row', split_axis=0, concat_axis=2, tiled=True)  78.9 us
    all_gather x1, waiting for transfers between devices, body(): gathered = lax.all_gather(picked_cols, 'col', axis=1, tiled=True)  72.6 us
    dynamic_update_slice x10, local copies, waits for them, and re-layouts, left_step(): lax.dynamic_update_slice_in_dim(band_rows, result_rows, offset_row, 0)  40.8 us
    dot_general x10, matrix products, left_step(): jnp.dot(factor_now.T, window_rows, precision=lax.Precision.HIGHEST, prefe...  34.4 us
    dynamic_update_slice x10, matrix products, right_step(): lax.dynamic_update_slice_in_dim(band_cols, result_cols, offset_col, 1)  33.5 us
    dynamic_update_slice x10, local copies, waits for them, and re-layouts, right_step(): lax.dynamic_update_slice_in_dim(band_cols, result_cols, offset_col, 1)  28.8 us
    unnamed x2, other arithmetic  19.2 us
  transfers between devices with their start and end apart: 4, of which 3 were waited for; matrix products, arithmetic and copies ran while one was open for 12% of the time, Pallas kernels for 0%

commit v1 on v0

--- a/solution.py
+++ b/solution.py
@@ -80,7 +80,10 @@
     row_tiles = band_rows.reshape(span_tiles, tile_size, received.shape[2])
     send_valid, send_place = slot_order(first_tile, row_count, rows_each, span_tiles)
     backsend = jnp.where(send_valid[:, None, None], jnp.take(row_tiles, send_place, axis=0), 0.0)
-    returned = lax.all_to_all(backsend, "row", split_axis=0, concat_axis=2, tiled=True)
+    returned = jnp.concatenate(
+        lax.all_to_all(jnp.stack(jnp.split(backsend, lax.axis_size("row"), axis=0)), "row", 0, 0),
+        axis=2,
+    )
     for member in range(rows_each):
         local_tiles = jnp.where(
             row_valid[member],

time: 619 us -> 642 us (1.037)
  local copies, waits for them, and re-layouts: 173 us -> 212 us
  other arithmetic: 47.9 us -> 31.9 us
    unnamed x2 -> x0, other arithmetic: 19.2 us -> none
    unnamed x12 -> x16, local copies, waits for them, and re-layouts: 10.4 us -> 28.3 us
    slice x3 -> x4, local copies, waits for them, and re-layouts: 0.7 us -> 12.5 us  [body(): returned[member]]
    select_n x1, local copies, waits for them, and re-layouts: 9.21 us -> 18.6 us  [body(): jnp.where(row_valid[:, None, None], jnp.take(local_tiles, row_index, axis...]
    select_n x3, other arithmetic: 2.95 us -> 12.1 us  [body(): jnp.where(row_valid[member], lax.dynamic_update_index_in_dim(local_tiles,...]
    reshape x1 -> x0, local copies, waits for them, and re-layouts: 7.23 us -> none  [body(): local_tiles = matrix.reshape(row_cycles, tile_size, col_cycles * tile_size)]
    select_n x0 -> x1, local copies, waits for them, and re-layouts: none -> 6.59 us  [body(): jnp.where(row_valid[member], lax.dynamic_update_index_in_dim(local_tiles,...]
  transfers between devices with their start and end apart: 4 -> 4, of which waited for: 3 -> 3; matrix products, arithmetic and copies ran while one was open for 12% -> 11% of each run, Pallas kernels for 0% -> 0%
where the time goes in v1:
time: 642 us; the launch traced here: 638 us
  waiting for transfers between devices  267 us (42%)
  local copies, waits for them, and re-layouts  212 us (33%)
  matrix products  67.9 us (11%)
  other arithmetic  31.9 us (5%)
  loops' own time  23.8 us (4%)
  between operations  22.2 us (3%)
  starting transfers between devices  12.5 us (2%)
    all_to_all x1, waiting for transfers between devices, body(): lax.all_to_all(picked, 'row', split_axis=2, concat_axis=0, tiled=True)  115 us
    all_to_all x1, waiting for transfers between devices, body(): lax.all_to_all(jnp.stack(jnp.split(backsend, lax.axis_size('row'), axis=0...  78.7 us
    all_gather x1, waiting for transfers between devices, body(): gathered = lax.all_gather(picked_cols, 'col', axis=1, tiled=True)  72.8 us
    dynamic_update_slice x10, local copies, waits for them, and re-layouts, left_step(): lax.dynamic_update_slice_in_dim(band_rows, result_rows, offset_row, 0)  40.8 us
    dot_general x10, matrix products, left_step(): jnp.dot(factor_now.T, window_rows, precision=lax.Precision.HIGHEST, prefe...  34.4 us
    dynamic_update_slice x10, matrix products, right_step(): lax.dynamic_update_slice_in_dim(band_cols, result_cols, offset_col, 1)  33.5 us
    dynamic_update_slice x10, local copies, waits for them, and re-layouts, right_step(): lax.dynamic_update_slice_in_dim(band_cols, result_cols, offset_col, 1)  28.8 us
    unnamed x16, local copies, waits for them, and re-layouts  28.3 us
  transfers between devices with their start and end apart: 4, of which 3 were waited for; matrix products, arithmetic and copies ran while one was open for 11% of the time, Pallas kernels for 0%

profile of v1, /device:TPU:1, one launch (start us, length us, event | category | flops | bytes accessed | tf_op | source)
XLA Modules:
  0.0 637.8 jit_solution(7580161165661235801)
XLA Ops:
  9.9 14.8 %copy.34 = f32[3,1,128,32,1,128]{2,5,3,0,4,1:T(8,128)} copy(f32[3,1,128,32,1,128]{5,4,3,2,1,0:T(1,128)} %param.7) | data formatting | bytes 12582912 | tf_op args[0]
  24.7 6.4 %gather_fusion = f32[3,128,4096]{1,2,0:T(8,128)} fusion(f32[3,128,4096]{1,2,0:T(8,128)} %bitcast.103, s32[1024]{0:T(1024)S(1)} %pad_clamp_fusion.3), kind=kCustom, calls=%fused_computation | custom fusion | bytes 12582924 | tf_op jit(solution)/shard_map/jit(_take)/gather | solution.py:75
  31.1 3.5 select_select_fusion.1
  34.6 18.6 %copy.35 = f32[3,128,4096]{1,0,2:T(4,128)} copy(f32[3,128,4096]{1,2,0:T(8,128)S(1)} %select_select_fusion.1) | data formatting | bytes 12582912 | tf_op jit(solution)/shard_map/jit(_where)/select_n | solution.py:75
  53.2 7.5 %all-to-all-start = ((f32[3,128,4096]{1,0,2:T(4,128)}), f32[3,128,4096]{1,0,2:T(4,128)}, u32[]{:S(2)}, u32[]{:S(2)}) async-start(f32[3,128,4096]{1,0,2:T(4,128)} %copy.35), calls=%async_computation | async-start | bytes 16777216 | tf_op jit(solution)/shard_map/all_to_all | solution.py:76
  60.9 115.0 %all-to-all-done = f32[3,128,4096]{1,0,2:T(4,128)} async-done(((f32[3,128,4096]{1,0,2:T(4,128)}), f32[3,128,4096]{1,0,2:T(4,128)}, u32[]{:S(2)}, u32[]{:S(2)}) %all-to-all-start) | async-done | bytes 6291488 | tf_op jit(solution)/shard_map/all_to_all | solution.py:76
  175.9 6.5 %copy.36 = f32[3,128,4096]{1,2,0:T(8,128)} copy(f32[3,128,4096]{1,0,2:T(4,128)} %all-to-all-done) | data formatting | bytes 12582912 | tf_op jit(solution)/shard_map/all_to_all | solution.py:76
  182.3 6.6 %copy.37 = f32[8,3,128,512]{3,2,1,0:T(8,128)} copy(f32[8,3,128,512]{2,3,0,1:T(8,128)} %bitcast.106) | data formatting | bytes 12582912 | tf_op jit(solution)/shard_map/all_to_all | solution.py:76
  188.9 6.2 gather_fusion.1
  195.1 5.0 bitcast_select_fusion
  200.2 11.3 %copy.38 = f32[10,512,512]{2,1,0:T(8,128)} copy(f32[10,512,512]{1,2,0:T(8,128)} %all-gather.3.cloned.1.call-done) | data formatting | bytes 20971520 | tf_op jit(solution)/shard_map/while | solution.py:79
  211.5 92.3 %while.28 = (s32[]{:T(128)}, f32[2816,512]{1,0:T(8,128)}, f32[10,512,512]{2,1,0:T(8,128)}, s32[10]{0:T(128)S(1)}, s32[]{:T(128)}, /*index=5*/s32[]{:T(128)}, s32[]{:T(128)}) while((s32[]{:T(128)}, f32[2816,512]{1,0:T(8,128)}, f32[10,512,512]{2,1,0:T(8,128)}, s32[10]{0:T(128)S(1)}, s32[]{:T(128)}, /*index=5*/s32[]{:T(128)}, s32[]{:T(128)}) %tuple.92), condition=%wide.region_1.2_spmd, body=%wide.region_0.1_spmd.sunk | while | flops 1610612736 | bytes 5243543 | solution.py:79
  213.2 3.4 fusion.55
  216.6 4.1 dynamic_update_slice.22
  222.5 3.4 fusion.55
  225.9 4.1 dynamic_update_slice.22
  231.7 3.4 fusion.55
  235.2 4.2 dynamic_update_slice.22
  241.0 3.4 fusion.55
  244.5 4.2 dynamic_update_slice.22
  250.3 3.4 fusion.55
  253.8 4.1 dynamic_update_slice.22
  259.6 3.4 fusion.55
  263.0 4.2 dynamic_update_slice.22
  268.9 3.4 fusion.55
  272.4 4.1 dynamic_update_slice.22
  278.2 3.5 fusion.55
  281.7 4.2 dynamic_update_slice.22
  287.5 3.5 fusion.55
  291.0 4.1 dynamic_update_slice.22
  296.9 3.4 fusion.55
  300.3 3.5 dynamic_update_slice.22
  303.8 6.2 gather_fusion.2
  310.0 4.1 select_select_fusion
  321.7 4.8 all-to-all-start.1
  334.1 78.7 %all-to-all-done.1 = f32[8,3,128,512]{3,2,1,0:T(8,128)} async-done(((f32[8,3,128,512]{3,2,1,0:T(8,128)}), f32[8,3,128,512]{3,2,1,0:T(8,128)}, u32[]{:S(2)}, u32[]{:S(2)}) %all-to-all-start.1) | async-done | bytes 6291488 | tf_op jit(solution)/shard_map/all_to_all | solution.py:84
  412.9 5.9 fusion.41
  418.7 2.9 copy.39
  425.4 4.6 constant_dynamic-update-slice_fusion.2
  430.0 3.7 constant_dynamic-update-slice_fusion.1
  433.7 3.8 constant_dynamic-update-slice_fusion
  437.5 6.6 %copy.42 = f32[3,128,4096]{2,1,0:T(8,128)} copy(f32[3,128,4096]{1,2,0:T(8,128)} %constant_dynamic-update-slice_fusion) | data formatting | bytes 12582912 | tf_op jit(solution)/shard_map/jit(_where)/select_n | solution.py:88
  444.1 4.1 copy.54
  451.9 72.8 %all-gather.5.cloned.1.call-done = f32[384,32,128]{2,0,1:T(8,128)} async-done(((f32[384,1,128]{2,0,1:T(8,128)}), f32[384,32,128]{2,0,1:T(8,128)}) %all-gather.5.cloned.1.call-update) | async-done | bytes 6291472 | tf_op jit(solution)/shard_map/all_gather | solution.py:99
  524.8 5.6 gather_fusion.3
  530.3 5.9 copy.44
  536.2 4.4 bitcast_select_fusion.1
  540.6 81.3 %while.29 = (s32[]{:T(128)}, f32[384,2816]{0,1:T(8,128)}, s32[10]{0:T(128)S(1)}, f32[10,512,512]{2,1,0:T(8,128)}, s32[]{:T(128)}, /*index=5*/s32[]{:T(128)}, s32[]{:T(128)}) while((s32[]{:T(128)}, f32[384,2816]{0,1:T(8,128)}, s32[10]{0:T(128)S(1)}, f32[10,512,512]{2,1,0:T(8,128)}, s32[]{:T(128)}, /*index=5*/s32[]{:T(128)}, s32[]{:T(128)}) %tuple.93), condition=%wide.region_3.4_spmd, body=%wide.region_2.3_spmd.sunk | while | flops 1207959552 | bytes 4194967 | solution.py:101
  542.5 3.3 fusion.59
  545.9 2.9 dynamic_update_slice.23
  550.7 3.3 fusion.59
  558.8 3.3 fusion.59
  566.9 3.3 fusion.59
  570.2 2.9 dynamic_update_slice.23
  575.0 3.3 fusion.59
  578.4 2.9 dynamic_update_slice.23
  583.2 3.3 fusion.59
  586.5 2.9 dynamic_update_slice.23
  591.3 3.3 fusion.59
  599.4 3.3 fusion.59
  607.6 3.3 fusion.59
  615.7 3.3 fusion.59
  619.0 2.9 dynamic_update_slice.23
  624.6 6.4 select_n.478
  (65 shorter events, 46.9 us)
Async XLA Ops:
  6.5 193.6 %all-gather.3.cloned.1.call-start = ((), (), s32[]{:S(2)}) async-start(), calls=%async_computation.2 | async-start | bytes 10813440 | tf_op jit(solution)/shard_map/all_gather | solution.py:46
  53.2 122.6 %all-to-all-start = ((f32[3,128,4096]{1,0,2:T(4,128)}), f32[3,128,4096]{1,0,2:T(4,128)}, u32[]{:S(2)}, u32[]{:S(2)}) async-start(f32[3,128,4096]{1,0,2:T(4,128)} %copy.35), calls=%async_computation | async-start | bytes 16777216 | tf_op jit(solution)/shard_map/all_to_all | solution.py:76
  200.2 11.3 %copy-start.2 = (s32[10]{0:T(128)S(1)}, s32[10]{0:T(128)}, u32[]{:S(2)}) copy-start(s32[10]{0:T(128)} %param.9) | copy-start | bytes 124
  321.7 91.2 %all-to-all-start.1 = ((f32[8,3,128,512]{3,2,1,0:T(8,128)}), f32[8,3,128,512]{3,2,1,0:T(8,128)}, u32[]{:S(2)}, u32[]{:S(2)}) async-start(f32[8,3,128,512]{3,2,1,0:T(8,128)} %fusion.10), calls=%async_computation.1 | async-start | bytes 12582912 | tf_op jit(solution)/shard_map/all_to_all | solution.py:84
  326.5 198.3 %all-gather.5.cloned.1.call-start = ((), (), s32[]{:S(2)}) async-start(), calls=%async_computation.3 | async-start | bytes 6488064 | tf_op jit(solution)/shard_map/all_gather | solution.py:99
  425.3 4.6 copy-start
  448.2 2.7 copy-start.1
Sparse Core Ops, SparseCore 0:
  9.2 165.0 all-gather.2
  451.9 72.8 all-gather.4
